TPU v7x, 128 devices: a whole 4x4x4 slice. The times are simulated.
128 devices in a mesh: ep: 16 (over x, z), tp: 8 (over y, core).
Axes of the slice: x: 4, y: 4, z: 4, core: 2. Of those that a mesh axis runs over, the one named last changes fastest.
Arguments:
- tokens: bfloat16 [2048, 4096], P('ep', 'tp'), may hold values from -6 to 6
- out_grad: bfloat16 [2048, 4096], P('ep', 'tp'), may hold values from -6 to 6
- routes: int32 [2048, 4], P('ep'), may hold values from 0 to 15, all different within a row; in each aligned block of 128 rows (0 to 127, 128 to 255, ...) at most 64 rows name the same one
- probs: bfloat16 [2048, 4], P('ep'), may hold values from 0.019897461 to 0.59765625
- w_in: bfloat16 [16, 2, 1536, 4096], P('ep', None, 'tp'), as said below
- w_out: bfloat16 [16, 1536, 4096], P('ep', 'tp'), as said below
Outputs:
- in_grad: bfloat16 [2048, 4096], P('ep', 'tp')
- grad_in: bfloat16 [16, 2, 1536, 4096], P('ep', None, 'tp')
- grad_out: bfloat16 [16, 1536, 4096], P('ep', 'tp')
Inputs may be any that keep to these rules, and one draw needn't show every extreme that they name: `routes`: each token names 4 different copies; within the tokens of one device (aligned blocks of 128 tokens) no copy is named more than 64 times, a bound that some block reaches. `w_in`: copies c and c + 8 hold equal weights. `w_out`: copies c and c + 8 hold equal weights.
All inputs are finite; a program needn't handle non-finite values.
Results may differ from a plain program's by a relative error of at most 0.02.
Values may be sent and summed in bfloat16 or wider, within the bound.
A program may use at most 128 MiB of HBM per device.

v0:
```python
import jax
import jax.numpy as jnp
from jax import lax
from jax.sharding import PartitionSpec as P


def partner(block, axis, apart):
    count = lax.axis_size(axis)
    route = []
    for low in range(count):
        high = low | 1 << apart
        if high != low and high < count:
            route += [(low, high), (high, low)]
    return lax.ppermute(block, axis, route)


def slot_tables(block_routes, copies, cap):
    flat = block_routes.reshape(-1)
    nrows = flat.shape[0]
    onehot = (flat[:, None] == jnp.arange(copies, dtype=jnp.int32)[None, :]).astype(jnp.int32)
    ranks = jnp.sum((jnp.cumsum(onehot, axis=0) - 1) * onehot, axis=1)
    slot = flat * cap + ranks
    source = (
        jnp.full((copies * cap,), nrows, jnp.int32).at[slot].set(jnp.arange(nrows, dtype=jnp.int32))
    )
    return (slot, source)


def body(tokens, out_grad, routes, probs, w_in, w_out):
    n_ep = lax.axis_size("ep")
    tok_dev, top = routes.shape
    nrows = tok_dev * top
    cap = 2 * nrows // n_ep
    slot, source = slot_tables(routes, n_ep, cap)
    valid = source < nrows
    local = jnp.minimum(source, nrows - 1)
    tok_index = local // top
    scale = jnp.where(valid, probs.reshape(-1)[local].astype(jnp.float32), 0.0)[:, None]
    full_x, full_g = (
        lax.all_gather(tokens, "tp", axis=1, tiled=True),
        lax.all_gather(out_grad, "tp", axis=1, tiled=True),
    )
    packed_x = jnp.where(valid[:, None], full_x[tok_index], jnp.zeros((), jnp.bfloat16))
    packed_g = (scale * full_g[tok_index].astype(jnp.float32)).astype(jnp.bfloat16)
    width = full_x.shape[1]
    send_x = packed_x.reshape(n_ep, cap, width)
    send_g = packed_g.reshape(n_ep, cap, width)
    recv_x, recv_g = (
        lax.all_to_all(send_x, "ep", split_axis=0, concat_axis=0, tiled=True),
        lax.all_to_all(send_g, "ep", split_axis=0, concat_axis=0, tiled=True),
    )
    width = recv_x.shape[2]
    rows_x = recv_x.reshape(n_ep * cap, width)
    rows_g = recv_g.reshape(n_ep * cap, width)
    w_gate = w_in[0, 0]
    w_up = w_in[0, 1]
    w_down = w_out[0]
    contract_last = (((1,), (1,)), ((), ()))
    a = lax.dot_general(rows_x, w_gate, contract_last, preferred_element_type=jnp.float32)
    b = lax.dot_general(rows_x, w_up, contract_last, preferred_element_type=jnp.float32)
    sig = jax.nn.sigmoid(a)
    silu = a * sig
    hidden = (silu * b).astype(jnp.bfloat16)
    dh = lax.dot_general(rows_g, w_down, contract_last, preferred_element_type=jnp.float32)
    da = (dh * b * sig * (1.0 + a * (1.0 - sig))).astype(jnp.bfloat16)
    db = (dh * silu).astype(jnp.bfloat16)
    partial_rows = jnp.dot(da, w_gate, preferred_element_type=jnp.float32)
    partial_rows = partial_rows + jnp.dot(db, w_up, preferred_element_type=jnp.float32)
    summed = lax.psum_scatter(
        partial_rows.reshape(n_ep, cap, width).astype(jnp.bfloat16),
        "tp",
        scatter_dimension=2,
        tiled=True,
    )
    back = lax.all_to_all(summed, "ep", split_axis=0, concat_axis=0, tiled=True)
    picked = back.reshape(n_ep * cap, back.shape[2])[slot]
    in_grad = jnp.sum(
        picked.astype(jnp.float32).reshape(tok_dev, top, back.shape[2]), axis=1
    ).astype(jnp.bfloat16)
    contract_rows = (((0,), (0,)), ((), ()))
    own_in = jnp.stack(
        [
            lax.dot_general(da, rows_x, contract_rows, preferred_element_type=jnp.float32),
            lax.dot_general(db, rows_x, contract_rows, preferred_element_type=jnp.float32),
        ]
    ).astype(jnp.bfloat16)[None]
    own_out = lax.dot_general(
        hidden, rows_g, contract_rows, preferred_element_type=jnp.float32
    ).astype(jnp.bfloat16)[None]
    half_bit = n_ep.bit_length() - 2
    other_in, other_out = partner((own_in, own_out), "ep", half_bit)
    grad_in = (own_in.astype(jnp.float32) + other_in.astype(jnp.float32)).astype(jnp.bfloat16)
    grad_out = (own_out.astype(jnp.float32) + other_out.astype(jnp.float32)).astype(jnp.bfloat16)
    return (in_grad, grad_in, grad_out)


def solution(mesh):
    return jax.shard_map(
        body,
        mesh=mesh,
        in_specs=(
            P("ep", "tp"),
            P("ep", "tp"),
            P("ep", None),
            P("ep", None),
            P("ep", None, "tp", None),
            P("ep", "tp", None),
        ),
        out_specs=(P("ep", "tp"), P("ep", None, "tp", None), P("ep", "tp", None)),
        check_vma=False,
    )
```

profile of v0, /device:TPU:0, one launch (start us, length us, event | category | flops | bytes accessed | tf_op | source)
XLA Modules:
  0.0 534.7 jit_solution(16174911186118901653)
XLA Ops:
  7.2 0.7 all-gather.5.cloned.1.call-update
  7.9 0.8 copy.10
  8.7 0.1 eq.29
  8.8 0.1 eq.25
  8.9 1.2 reduce-window.6
  10.1 0.2 slice_reduce_fusion
  10.3 0.7 broadcast_multiply_fusion
  11.0 0.1 copy.9
  11.2 0.1 mul.53
  11.3 0.8 copy.13
  12.1 0.1 reshape.144
  12.2 0.1 fusion.20
  12.3 2.4 scatter_custom_fusion
  14.8 6.8 %gather_fusion = bf16[1024]{0:T(1024)(128)(2,1)S(1)} fusion(bf16[512]{0:T(512)(128)(2,1)S(1)} %reshape.144, s32[1024]{0:T(1024)S(1)} %get-tuple-element.7), kind=kCustom, calls=%fused_computation | custom fusion | bytes 8192 | tf_op jit(solution)/shard_map/gather | solution.py:38
  21.6 0.1 broadcast_in_dim.35
  21.7 13.9 %all-gather.5.cloned.1.call-done = bf16[128,4096]{1,0:T(8,128)(2,1)} async-done(((bf16[128,512]{1,0:T(8,128)(2,1)}), bf16[128,4096]{1,0:T(8,128)(2,1)}) %all-gather.5.cloned.1.call-update) | async-done | bytes 1048592 | tf_op jit(solution)/shard_map/all_gather | solution.py:40
  35.6 16.4 %gather_fusion.2 = bf16[1024,4096]{1,0:T(8,128)(2,1)} fusion(bf16[128,4096]{1,0:T(8,128)(2,1)} %all-gather.5.cloned.1.call-done, s32[1024]{0:T(1024)S(1)} %get-tuple-element.8), kind=kCustom, calls=%fused_computation.2 | custom fusion | bytes 16781312 | tf_op jit(solution)/shard_map/gather | solution.py:43
  52.0 7.2 %broadcast_select_fusion = bf16[16,64,4096]{2,1,0:T(8,128)(2,1)} fusion(bf16[16,64,4096]{2,1,0:T(8,128)(2,1)} %bitcast.56, pred[16,64]{1,0:T(8,128)(4,1)S(1)} %broadcast_in_dim.35), kind=kLoop, calls=%fused_computation.8 | loop fusion | flops 4194304 | bytes 16778240 | tf_op jit(solution)/shard_map/jit(_where)/select_n | solution.py:43
  59.2 7.0 %all-to-all-start.1 = ((bf16[16,64,4096]{2,1,0:T(8,128)(2,1)}), bf16[16,64,4096]{2,1,0:T(8,128)(2,1)}, u32[]{:S(2)}, u32[]{:S(2)}) async-start(bf16[16,64,4096]{2,1,0:T(8,128)(2,1)} %broadcast_select_fusion), calls=%async_computation.1 | async-start | bytes 16777216 | tf_op jit(solution)/shard_map/all_to_all | solution.py:49
  66.3 0.0 all-gather.3.cloned.1.call-start
  66.3 0.7 all-gather.3.cloned.1.call-update
  67.0 0.1 mul.55
  67.1 25.2 %all-gather.3.cloned.1.call-done = bf16[128,4096]{1,0:T(8,128)(2,1)} async-done(((bf16[128,512]{1,0:T(8,128)(2,1)}), bf16[128,4096]{1,0:T(8,128)(2,1)}) %all-gather.3.cloned.1.call-update) | async-done | bytes 1048592 | tf_op jit(solution)/shard_map/all_gather | solution.py:41
  92.3 16.4 %gather_fusion.1 = bf16[1024,4096]{1,0:T(8,128)(2,1)} fusion(bf16[128,4096]{1,0:T(8,128)(2,1)} %all-gather.3.cloned.1.call-done, s32[1024]{0:T(1024)S(1)} %get-tuple-element.8), kind=kCustom, calls=%fused_computation.1 | custom fusion | bytes 16781312 | tf_op jit(solution)/shard_map/gather | solution.py:44
  108.7 10.0 %fusion = bf16[16,64,4096]{2,1,0:T(8,128)(2,1)} fusion(bf16[16,64,4096]{2,1,0:T(8,128)(2,1)} %bitcast.57, f32[16,64]{1,0:T(8,128)S(1)} %mul.55), kind=kLoop, calls=%fused_computation.6 | loop fusion | flops 12582912 | bytes 16781312 | tf_op jit(solution)/shard_map/convert_element_type | solution.py:44
  118.7 93.8 %all-to-all-done.1 = bf16[16,64,4096]{2,1,0:T(8,128)(2,1)} async-done(((bf16[16,64,4096]{2,1,0:T(8,128)(2,1)}), bf16[16,64,4096]{2,1,0:T(8,128)(2,1)}, u32[]{:S(2)}, u32[]{:S(2)}) %all-to-all-start.1) | async-done | bytes 8388640 | tf_op jit(solution)/shard_map/all_to_all | solution.py:49
  212.5 11.8 %all-to-all-start = ((bf16[16,64,4096]{2,1,0:T(8,128)(2,1)}), bf16[16,64,4096]{2,1,0:T(8,128)(2,1)}, u32[]{:S(2)}, u32[]{:S(2)}) async-start(bf16[16,64,4096]{2,1,0:T(8,128)(2,1)} %fusion), calls=%async_computation | async-start | bytes 16777216 | tf_op jit(solution)/shard_map/all_to_all | solution.py:50
  224.3 0.2 reduce-scatter.2.cloned.1.call-start
  224.5 6.8 %fusion.6 = f32[1024,192]{0,1:T(8,128)S(1)} fusion(bf16[1024,4096]{1,0:T(8,128)(2,1)} %bitcast.7, bf16[1,2,192,4096]{3,2,1,0:T(8,128)(2,1)} %param.10), kind=kOutput, calls=%fused_computation.20 | convolution fusion | flops 1610612736 | bytes 10747904 | tf_op jit(solution)/shard_map/dot_general | solution.py:59
  231.4 7.2 %fusion.9 = f32[1024,192]{0,1:T(8,128)} fusion(bf16[1024,4096]{1,0:T(8,128)(2,1)} %bitcast.7, bf16[1,2,192,4096]{3,2,1,0:T(8,128)(2,1)S(1)} %copy-done.3), kind=kOutput, calls=%fused_computation.23 | convolution fusion | flops 1610612736 | bytes 10747904 | tf_op jit(solution)/shard_map/dot_general | solution.py:60
  238.5 119.4 %all-to-all-done = bf16[16,64,4096]{2,1,0:T(8,128)(2,1)} async-done(((bf16[16,64,4096]{2,1,0:T(8,128)(2,1)}), bf16[16,64,4096]{2,1,0:T(8,128)(2,1)}, u32[]{:S(2)}, u32[]{:S(2)}) %all-to-all-start) | async-done | bytes 8388640 | tf_op jit(solution)/shard_map/all_to_all | solution.py:50
  357.9 6.7 %multiply_convert_fusion.1 = (bf16[1024,192]{0,1:T(8,128)(2,1)S(1)}, bf16[1024,192]{0,1:T(8,128)(2,1)S(1)}) fusion(f32[1024,192]{0,1:T(8,128)S(1)} %fusion.6, f32[1024,192]{0,1:T(8,128)} %fusion.9, bf16[1024,4096]{1,0:T(8,128)(2,1)} %bitcast.4, bf16[1,192,4096]{2,1,0:T(8,128)(2,1)S(1)} %copy-done), kind=kOutput, calls=%fused_computation.32 | convolution fusion | flops 1613168640 | bytes 12320768 | tf_op jit(solution)/shard_map/dot_general | solution.py:64
  364.6 8.1 %fusion.4 = f32[1024,4096]{1,0:T(8,128)} fusion(bf16[1024,192]{0,1:T(8,128)(2,1)S(1)} %get-tuple-element.6, bf16[1,2,192,4096]{3,2,1,0:T(8,128)(2,1)S(1)} %copy-done.4), kind=kOutput, calls=%fused_computation.18 | convolution fusion | flops 1610612736 | bytes 18743296 | tf_op jit(solution)/shard_map/dot_general | solution.py:67
  372.8 11.4 %add_convert_fusion = bf16[1024,4096]{1,0:T(8,128)(2,1)} fusion(f32[1024,4096]{1,0:T(8,128)} %fusion.4, bf16[1024,192]{0,1:T(8,128)(2,1)S(1)} %get-tuple-element.5, bf16[1,2,192,4096]{3,2,1,0:T(8,128)(2,1)S(1)} %copy-done.4), kind=kOutput, calls=%fused_computation.7 | convolution fusion | flops 1619001344 | bytes 27131904 | tf_op jit(solution)/shard_map/dot_general | solution.py:68
  384.2 5.4 %fusion.1 = bf16[1,1,192,4096]{3,2,1,0:T(8,128)(2,1)S(1)} fusion(bf16[1024,192]{0,1:T(8,128)(2,1)S(1)} %get-tuple-element.6, bf16[1024,4096]{1,0:T(8,128)(2,1)} %bitcast.7), kind=kOutput, calls=%fused_computation.13 | convolution fusion | flops 1611399168 | bytes 10354688 | tf_op jit(solution)/shard_map/dot_general | solution.py:83
  389.7 5.8 %fusion.2 = bf16[1,1,192,4096]{3,2,1,0:T(8,128)(2,1)S(1)} fusion(bf16[1024,192]{0,1:T(8,128)(2,1)S(1)} %get-tuple-element.5, bf16[1024,4096]{1,0:T(8,128)(2,1)} %bitcast.7), kind=kOutput, calls=%fused_computation.14 | convolution fusion | flops 1611399168 | bytes 10354688 | tf_op jit(solution)/shard_map/dot_general | solution.py:84
  395.4 1.9 pad_maximum_fusion
  397.4 0.2 copy-done.2
  397.6 5.3 fusion.3
  402.9 3.7 collective-permute-start.1
  406.6 92.6 %collective-permute-done.1 = bf16[1,192,4096]{2,1,0:T(8,128)(2,1)S(1)} collective-permute-done((bf16[1,192,4096]{2,1,0:T(8,128)(2,1)S(1)}, bf16[1,192,4096]{2,1,0:T(8,128)(2,1)S(1)}, u32[]{:S(2)}, u32[]{:S(2)}) %collective-permute-start.1) | collective-permute-done | bytes 1572896 | tf_op jit(solution)/shard_map/ppermute | solution.py:14
  499.2 1.7 add_convert_fusion.2
  500.9 9.9 %all-to-all-start.2 = ((bf16[16,64,512]{2,1,0:T(8,128)(2,1)}), bf16[16,64,512]{2,1,0:T(8,128)(2,1)S(1)}, u32[]{:S(2)}, u32[]{:S(2)}) async-start(bf16[16,64,512]{2,1,0:T(8,128)(2,1)} %reduce-scatter.2.cloned.1.call-done), calls=%async_computation.3 | async-start | bytes 2097152 | tf_op jit(solution)/shard_map/all_to_all | solution.py:75
  510.8 5.8 %add_convert_fusion.1 = bf16[1,2,192,4096]{3,2,1,0:T(8,128)(2,1)} fusion(bf16[1,2,192,4096]{3,2,1,0:T(8,128)(2,1)} %collective-permute-done, bf16[1,1,192,4096]{3,2,1,0:T(8,128)(2,1)} %copy-done.2, bf16[1,1,192,4096]{3,2,1,0:T(8,128)(2,1)} %copy-done.1), kind=kLoop, calls=%fused_computation.9 | loop fusion | flops 7864320 | bytes 9437184 | tf_op jit(solution)/shard_map/convert_element_type | solution.py:92
  516.6 8.2 %all-to-all-done.2 = bf16[16,64,512]{2,1,0:T(8,128)(2,1)S(1)} async-done(((bf16[16,64,512]{2,1,0:T(8,128)(2,1)}), bf16[16,64,512]{2,1,0:T(8,128)(2,1)S(1)}, u32[]{:S(2)}, u32[]{:S(2)}) %all-to-all-start.2) | async-done | bytes 1048608 | tf_op jit(solution)/shard_map/all_to_all | solution.py:75
  524.7 2.0 gather_fusion.3
  526.7 0.1 gather.21
  526.8 1.3 reduce_sum.25
  (24 shorter events, 0.2 us)
Async XLA Ops:
  7.2 350.7 %copy-start = (bf16[1,192,4096]{2,1,0:T(8,128)(2,1)S(1)}, bf16[1,192,4096]{2,1,0:T(8,128)(2,1)}, u32[]{:S(2)}) copy-start(bf16[1,192,4096]{2,1,0:T(8,128)(2,1)} %param.11) | copy-start | bytes 4718596
  7.2 28.4 %all-gather.5.cloned.1.call-start = ((), (), s32[]{:S(2)}) async-start(), calls=%async_computation.5 | async-start | bytes 1179648 | tf_op jit(solution)/shard_map/all_gather | solution.py:40
  59.2 153.3 %all-to-all-start.1 = ((bf16[16,64,4096]{2,1,0:T(8,128)(2,1)}), bf16[16,64,4096]{2,1,0:T(8,128)(2,1)}, u32[]{:S(2)}, u32[]{:S(2)}) async-start(bf16[16,64,4096]{2,1,0:T(8,128)(2,1)} %broadcast_select_fusion), calls=%async_computation.1 | async-start | bytes 16777216 | tf_op jit(solution)/shard_map/all_to_all | solution.py:49
  66.3 26.0 %all-gather.3.cloned.1.call-start = ((), (), s32[]{:S(2)}) async-start(), calls=%async_computation.4 | async-start | bytes 1179648 | tf_op jit(solution)/shard_map/all_gather | solution.py:41
  212.5 145.4 %all-to-all-start = ((bf16[16,64,4096]{2,1,0:T(8,128)(2,1)}), bf16[16,64,4096]{2,1,0:T(8,128)(2,1)}, u32[]{:S(2)}, u32[]{:S(2)}) async-start(bf16[16,64,4096]{2,1,0:T(8,128)(2,1)} %fusion), calls=%async_computation | async-start | bytes 16777216 | tf_op jit(solution)/shard_map/all_to_all | solution.py:50
  224.3 276.6 %reduce-scatter.2.cloned.1.call-start = ((), (), s32[]{:S(2)}) async-start(), calls=%async_computation.6 | async-start | bytes 9437184 | tf_op jit(solution)/shard_map/reduce_scatter | solution.py:69
  224.5 6.9 %copy-start.3 = (bf16[1,2,192,4096]{3,2,1,0:T(8,128)(2,1)S(1)}, bf16[1,2,192,4096]{3,2,1,0:T(8,128)(2,1)}, u32[]{:S(2)}) copy-start(bf16[1,2,192,4096]{3,2,1,0:T(8,128)(2,1)} %param.10) | copy-start | bytes 9437188
  357.9 6.7 %copy-start.4 = (bf16[1,2,192,4096]{3,2,1,0:T(8,128)(2,1)S(1)}, bf16[1,2,192,4096]{3,2,1,0:T(8,128)(2,1)}, u32[]{:S(2)}) copy-start(bf16[1,2,192,4096]{3,2,1,0:T(8,128)(2,1)} %param.10) | copy-start | bytes 9437188
  389.6 5.8 %copy-start.1 = (bf16[1,1,192,4096]{3,2,1,0:T(8,128)(2,1)}, bf16[1,1,192,4096]{3,2,1,0:T(8,128)(2,1)S(1)}, u32[]{:S(2)}) copy-start(bf16[1,1,192,4096]{3,2,1,0:T(8,128)(2,1)S(1)} %fusion.1) | copy-start | bytes 4718596
  395.4 2.2 copy-start.2
  395.4 2.2 copy-start.5
  397.6 113.2 %collective-permute-start = (bf16[1,2,192,4096]{3,2,1,0:T(8,128)(2,1)}, bf16[1,2,192,4096]{3,2,1,0:T(8,128)(2,1)}, u32[]{:S(2)}, u32[]{:S(2)}) collective-permute-start(bf16[1,2,192,4096]{3,2,1,0:T(8,128)(2,1)} %pad_maximum_fusion), channel_id=1, source_target_pairs={{0,64},{64,0},{8,72},{72,8},{16,80},{80,16},{24,88},{88,24},{32,96... | collective-permute-start | bytes 9437192 | tf_op jit(solution)/shard_map/ppermute | solution.py:14
  402.9 96.3 %collective-permute-start.1 = (bf16[1,192,4096]{2,1,0:T(8,128)(2,1)S(1)}, bf16[1,192,4096]{2,1,0:T(8,128)(2,1)S(1)}, u32[]{:S(2)}, u32[]{:S(2)}) collective-permute-start(bf16[1,192,4096]{2,1,0:T(8,128)(2,1)S(1)} %fusion.3), channel_id=1, source_target_pairs={{0,64},{64,0},{8,72},{72,8},{16,80},{80,16},{24,88},{88,24},{32,96... | collective-permute-start | bytes 4718600 | tf_op jit(solution)/shard_map/ppermute | solution.py:14
  500.9 23.9 %all-to-all-start.2 = ((bf16[16,64,512]{2,1,0:T(8,128)(2,1)}), bf16[16,64,512]{2,1,0:T(8,128)(2,1)S(1)}, u32[]{:S(2)}, u32[]{:S(2)}) async-start(bf16[16,64,512]{2,1,0:T(8,128)(2,1)} %reduce-scatter.2.cloned.1.call-done), calls=%async_computation.3 | async-start | bytes 2097152 | tf_op jit(solution)/shard_map/all_to_all | solution.py:75
Sparse Core Ops, SparseCore 0:
  9.7 25.8 all-gather.4
  68.8 23.4 all-gather.2
  384.3 54.3 reduce-scatter.1
where the time goes:
time: 535 us
  waiting for transfers between devices  354 us (66%)
  matrix products  56.7 us (11%)
  local copies, waits for them, and re-layouts  47 us (9%)
  starting transfers between devices  32.6 us (6%)
  other arithmetic  30 us (6%)
  between operations  14 us (3%)
    all_to_all x1, waiting for transfers between devices, body(): lax.all_to_all(send_g, 'ep', split_axis=0, concat_axis=0, tiled=True)  119 us
    all_to_all x1, waiting for transfers between devices, body(): lax.all_to_all(send_x, 'ep', split_axis=0, concat_axis=0, tiled=True)  93.8 us
    ppermute x2, waiting for transfers between devices, partner(): return lax.ppermute(block, axis, route)  92.6 us
    all_gather x1, waiting for transfers between devices, body(): lax.all_gather(out_grad, 'tp', axis=1, tiled=True)  25.2 us
    gather x1, local copies, waits for them, and re-layouts, body(): full_g[tok_index].astype(jnp.float32)  16.4 us
    gather x1, local copies, waits for them, and re-layouts, body(): full_x[tok_index]  16.4 us
    all_gather x1, waiting for transfers between devices, body(): lax.all_gather(tokens, 'tp', axis=1, tiled=True)  13.9 us
    all_to_all x1, starting transfers between devices, body(): lax.all_to_all(send_g, 'ep', split_axis=0, concat_axis=0, tiled=True)  11.8 us
  transfers between devices with their start and end apart: 8, of which 6 were waited for; matrix products, arithmetic and copies ran while one was open for 15% of the time, Pallas kernels for 0%

commit v1 on v0

--- a/solution.py
+++ b/solution.py
@@ -1,7 +1,18 @@
+import functools
 import jax
 import jax.numpy as jnp
 from jax import lax
 from jax.sharding import PartitionSpec as P
+from jax.lax import all_to_all, axis_size
+
+
+def watch_values_on_mesh(chunk, comm_axis):
+    return jnp.concatenate(
+        all_to_all(jnp.stack(axis_size(comm_axis) * [chunk]), comm_axis, 0, 0), axis=1
+    )
+
+
+thing_compute = functools.partial(watch_values_on_mesh, comm_axis="tp")
 
 
 def partner(block, axis, apart):
@@ -36,10 +47,7 @@
     local = jnp.minimum(source, nrows - 1)
     tok_index = local // top
     scale = jnp.where(valid, probs.reshape(-1)[local].astype(jnp.float32), 0.0)[:, None]
-    full_x, full_g = (
-        lax.all_gather(tokens, "tp", axis=1, tiled=True),
-        lax.all_gather(out_grad, "tp", axis=1, tiled=True),
-    )
+    full_x, full_g = (thing_compute(tokens), lax.all_gather(out_grad, "tp", axis=1, tiled=True))
     packed_x = jnp.where(valid[:, None], full_x[tok_index], jnp.zeros((), jnp.bfloat16))
     packed_g = (scale * full_g[tok_index].astype(jnp.float32)).astype(jnp.bfloat16)
     width = full_x.shape[1]

time: 535 us -> 518 us (0.968)
  the two profiles are of different devices: /device:TPU:0 before, /device:TPU:16 now
where the time goes in v1:
time: 518 us; the launch traced here: 517 us
  waiting for transfers between devices  341 us (66%)
  matrix products  56.8 us (11%)
  local copies, waits for them, and re-layouts  41.5 us (8%)
  starting transfers between devices  33.8 us (7%)
  other arithmetic  29.3 us (6%)
  between operations  14.3 us (3%)
    all_to_all x1, waiting for transfers between devices, body(): lax.all_to_all(send_g, 'ep', split_axis=0, concat_axis=0, tiled=True)  119 us
    all_to_all x1, waiting for transfers between devices, body(): lax.all_to_all(send_x, 'ep', split_axis=0, concat_axis=0, tiled=True)  94 us
    ppermute x2, waiting for transfers between devices, partner(): return lax.ppermute(block, axis, route)  92.2 us
    all_gather x1, waiting for transfers between devices, body(): lax.all_gather(out_grad, 'tp', axis=1, tiled=True)  26 us
    gather x1, local copies, waits for them, and re-layouts, body(): full_g[tok_index].astype(jnp.float32)  16.4 us
    dot_general x1, matrix products, body(): jnp.dot(db, w_up, preferred_element_type=jnp.float32)  11.4 us
  transfers between devices with their start and end apart: 8, of which 6 were waited for; matrix products, arithmetic and copies ran while one was open for 15% of the time, Pallas kernels for 0%

profile of v1, /device:TPU:16, one launch (start us, length us, event | category | flops | bytes accessed | tf_op | source)
XLA Modules:
  0.0 517.0 jit_solution(12348843069956194823)
XLA Ops:
  7.2 2.1 stack.8
  9.3 4.8 all-to-all-start.1
  14.1 0.1 copy.15
  14.2 0.1 eq.29
  14.3 0.1 eq.25
  14.4 1.2 reduce-window.6
  15.6 0.2 slice_reduce_fusion
  15.8 0.1 copy.14
  16.0 0.1 mul.53
  16.1 0.1 copy.18
  16.2 0.1 reshape.152
  16.3 0.1 fusion.20
  16.5 2.4 scatter_custom_fusion
  18.9 6.8 %gather_fusion = bf16[1024]{0:T(1024)(128)(2,1)S(1)} fusion(bf16[512]{0:T(512)(128)(2,1)S(1)} %reshape.152, s32[1024]{0:T(1024)S(1)} %get-tuple-element.7), kind=kCustom, calls=%fused_computation | custom fusion | bytes 8192 | tf_op jit(solution)/shard_map/gather | solution.py:49
  25.8 0.1 broadcast_in_dim.35
  25.8 1.1 all-to-all-done.1
  26.9 1.0 copy-done.3
  27.9 1.3 copy.21
  29.2 7.8 %gather_fusion.2 = bf16[1024,4096]{1,0:T(8,128)(2,1)} fusion(bf16[128,4096]{1,0:T(8,128)(2,1)S(1)} %bitcast.58, s32[1024]{0:T(1024)S(1)} %get-tuple-element.8), kind=kCustom, calls=%fused_computation.2 | custom fusion | bytes 16781312 | tf_op jit(solution)/shard_map/gather | solution.py:51
  37.0 7.2 %broadcast_select_fusion = bf16[16,64,4096]{2,1,0:T(8,128)(2,1)} fusion(bf16[16,64,4096]{2,1,0:T(8,128)(2,1)} %bitcast.60, pred[16,64]{1,0:T(8,128)(4,1)S(1)} %broadcast_in_dim.35), kind=kLoop, calls=%fused_computation.8 | loop fusion | flops 4194304 | bytes 16778240 | tf_op jit(solution)/shard_map/jit(_where)/select_n | solution.py:51
  44.2 7.9 %all-to-all-start.2 = ((bf16[16,64,4096]{2,1,0:T(8,128)(2,1)}), bf16[16,64,4096]{2,1,0:T(8,128)(2,1)}, u32[]{:S(2)}, u32[]{:S(2)}) async-start(bf16[16,64,4096]{2,1,0:T(8,128)(2,1)} %broadcast_select_fusion), calls=%async_computation.2 | async-start | bytes 16777216 | tf_op jit(solution)/shard_map/all_to_all | solution.py:57
  52.2 0.7 all-gather.2.cloned.1.call-update
  53.0 26.0 %all-gather.2.cloned.1.call-done = bf16[128,4096]{1,0:T(8,128)(2,1)} async-done(((bf16[128,512]{1,0:T(8,128)(2,1)}), bf16[128,4096]{1,0:T(8,128)(2,1)}) %all-gather.2.cloned.1.call-update) | async-done | bytes 1048592 | tf_op jit(solution)/shard_map/all_gather | solution.py:50
  79.0 16.4 %gather_fusion.1 = bf16[1024,4096]{1,0:T(8,128)(2,1)} fusion(bf16[128,4096]{1,0:T(8,128)(2,1)} %all-gather.2.cloned.1.call-done, s32[1024]{0:T(1024)S(1)} %get-tuple-element.8), kind=kCustom, calls=%fused_computation.1 | custom fusion | bytes 16781312 | tf_op jit(solution)/shard_map/gather | solution.py:52
  95.4 10.0 %fusion = bf16[16,64,4096]{2,1,0:T(8,128)(2,1)} fusion(bf16[16,64,4096]{2,1,0:T(8,128)(2,1)} %bitcast.61, f32[16,64]{1,0:T(8,128)S(1)} %mul.55), kind=kLoop, calls=%fused_computation.6 | loop fusion | flops 12582912 | bytes 16781312 | tf_op jit(solution)/shard_map/convert_element_type | solution.py:52
  105.4 94.0 %all-to-all-done.2 = bf16[16,64,4096]{2,1,0:T(8,128)(2,1)} async-done(((bf16[16,64,4096]{2,1,0:T(8,128)(2,1)}), bf16[16,64,4096]{2,1,0:T(8,128)(2,1)}, u32[]{:S(2)}, u32[]{:S(2)}) %all-to-all-start.2) | async-done | bytes 8388640 | tf_op jit(solution)/shard_map/all_to_all | solution.py:57
  199.4 8.4 %all-to-all-start = ((bf16[16,64,4096]{2,1,0:T(8,128)(2,1)}), bf16[16,64,4096]{2,1,0:T(8,128)(2,1)}, u32[]{:S(2)}, u32[]{:S(2)}) async-start(bf16[16,64,4096]{2,1,0:T(8,128)(2,1)} %fusion), calls=%async_computation | async-start | bytes 16777216 | tf_op jit(solution)/shard_map/all_to_all | solution.py:58
  207.8 0.2 reduce-scatter.2.cloned.1.call-start
  208.0 6.8 %fusion.6 = f32[1024,192]{0,1:T(8,128)S(1)} fusion(bf16[1024,4096]{1,0:T(8,128)(2,1)} %bitcast.8, bf16[1,2,192,4096]{3,2,1,0:T(8,128)(2,1)} %param.10), kind=kOutput, calls=%fused_computation.20 | convolution fusion | flops 1610612736 | bytes 10747904 | tf_op jit(solution)/shard_map/dot_general | solution.py:67
  214.9 7.2 %fusion.9 = f32[1024,192]{0,1:T(8,128)} fusion(bf16[1024,4096]{1,0:T(8,128)(2,1)} %bitcast.8, bf16[1,2,192,4096]{3,2,1,0:T(8,128)(2,1)S(1)} %copy-done.4), kind=kOutput, calls=%fused_computation.23 | convolution fusion | flops 1610612736 | bytes 10747904 | tf_op jit(solution)/shard_map/dot_general | solution.py:68
  222.0 119.4 %all-to-all-done = bf16[16,64,4096]{2,1,0:T(8,128)(2,1)} async-done(((bf16[16,64,4096]{2,1,0:T(8,128)(2,1)}), bf16[16,64,4096]{2,1,0:T(8,128)(2,1)}, u32[]{:S(2)}, u32[]{:S(2)}) %all-to-all-start) | async-done | bytes 8388640 | tf_op jit(solution)/shard_map/all_to_all | solution.py:58
  341.5 6.7 %multiply_convert_fusion.1 = (bf16[1024,192]{0,1:T(8,128)(2,1)S(1)}, bf16[1024,192]{0,1:T(8,128)(2,1)S(1)}) fusion(f32[1024,192]{0,1:T(8,128)S(1)} %fusion.6, f32[1024,192]{0,1:T(8,128)} %fusion.9, bf16[1024,4096]{1,0:T(8,128)(2,1)} %bitcast.4, bf16[1,192,4096]{2,1,0:T(8,128)(2,1)S(1)} %copy-done), kind=kOutput, calls=%fused_computation.32 | convolution fusion | flops 1613168640 | bytes 12320768 | tf_op jit(solution)/shard_map/dot_general | solution.py:72
  348.2 8.1 %fusion.4 = f32[1024,4096]{1,0:T(8,128)} fusion(bf16[1024,192]{0,1:T(8,128)(2,1)S(1)} %get-tuple-element.6, bf16[1,2,192,4096]{3,2,1,0:T(8,128)(2,1)S(1)} %copy-done.5), kind=kOutput, calls=%fused_computation.18 | convolution fusion | flops 1610612736 | bytes 18743296 | tf_op jit(solution)/shard_map/dot_general | solution.py:75
  356.4 11.4 %add_convert_fusion = bf16[1024,4096]{1,0:T(8,128)(2,1)} fusion(f32[1024,4096]{1,0:T(8,128)} %fusion.4, bf16[1024,192]{0,1:T(8,128)(2,1)S(1)} %get-tuple-element.5, bf16[1,2,192,4096]{3,2,1,0:T(8,128)(2,1)S(1)} %copy-done.5), kind=kOutput, calls=%fused_computation.7 | convolution fusion | flops 1619001344 | bytes 27131904 | tf_op jit(solution)/shard_map/dot_general | solution.py:76
  367.8 5.4 %fusion.1 = bf16[1,1,192,4096]{3,2,1,0:T(8,128)(2,1)S(1)} fusion(bf16[1024,192]{0,1:T(8,128)(2,1)S(1)} %get-tuple-element.6, bf16[1024,4096]{1,0:T(8,128)(2,1)} %bitcast.8), kind=kOutput, calls=%fused_computation.13 | convolution fusion | flops 1611399168 | bytes 10354688 | tf_op jit(solution)/shard_map/dot_general | solution.py:91
  373.2 5.8 %fusion.2 = bf16[1,1,192,4096]{3,2,1,0:T(8,128)(2,1)S(1)} fusion(bf16[1024,192]{0,1:T(8,128)(2,1)S(1)} %get-tuple-element.5, bf16[1024,4096]{1,0:T(8,128)(2,1)} %bitcast.8), kind=kOutput, calls=%fused_computation.14 | convolution fusion | flops 1611399168 | bytes 10354688 | tf_op jit(solution)/shard_map/dot_general | solution.py:92
  379.0 2.0 pad_maximum_fusion
  381.0 0.4 copy-done.2
  381.4 5.3 %fusion.3 = bf16[1,192,4096]{2,1,0:T(8,128)(2,1)S(1)} fusion(bf16[1024,4096]{1,0:T(8,128)(2,1)} %bitcast.4, f32[1024,192]{0,1:T(8,128)S(1)} %copy-done.8, f32[1024,192]{0,1:T(8,128)S(1)} %fusion.6), kind=kOutput, calls=%fused_computation.15 | convolution fusion | flops 1612578816 | bytes 11534336 | tf_op jit(solution)/shard_map/dot_general | solution.py:95
  386.7 3.6 collective-permute-start.1
  390.4 92.2 %collective-permute-done.1 = bf16[1,192,4096]{2,1,0:T(8,128)(2,1)S(1)} collective-permute-done((bf16[1,192,4096]{2,1,0:T(8,128)(2,1)S(1)}, bf16[1,192,4096]{2,1,0:T(8,128)(2,1)S(1)}, u32[]{:S(2)}, u32[]{:S(2)}) %collective-permute-start.1) | collective-permute-done | bytes 1572896 | tf_op jit(solution)/shard_map/ppermute | solution.py:25
  482.6 1.7 add_convert_fusion.2
  484.3 8.8 %all-to-all-start.3 = ((bf16[16,64,512]{2,1,0:T(8,128)(2,1)}), bf16[16,64,512]{2,1,0:T(8,128)(2,1)S(1)}, u32[]{:S(2)}, u32[]{:S(2)}) async-start(bf16[16,64,512]{2,1,0:T(8,128)(2,1)} %reduce-scatter.2.cloned.1.call-done), calls=%async_computation.4 | async-start | bytes 2097152 | tf_op jit(solution)/shard_map/all_to_all | solution.py:83
  493.1 5.8 %add_convert_fusion.1 = bf16[1,2,192,4096]{3,2,1,0:T(8,128)(2,1)} fusion(bf16[1,2,192,4096]{3,2,1,0:T(8,128)(2,1)} %collective-permute-done, bf16[1,1,192,4096]{3,2,1,0:T(8,128)(2,1)} %copy-done.2, bf16[1,1,192,4096]{3,2,1,0:T(8,128)(2,1)} %copy-done.1), kind=kLoop, calls=%fused_computation.9 | loop fusion | flops 7864320 | bytes 9437184 | tf_op jit(solution)/shard_map/convert_element_type | solution.py:100
  498.9 7.8 %all-to-all-done.3 = bf16[16,64,512]{2,1,0:T(8,128)(2,1)S(1)} async-done(((bf16[16,64,512]{2,1,0:T(8,128)(2,1)}), bf16[16,64,512]{2,1,0:T(8,128)(2,1)S(1)}, u32[]{:S(2)}, u32[]{:S(2)}) %all-to-all-start.3) | async-done | bytes 1048608 | tf_op jit(solution)/shard_map/all_to_all | solution.py:83
  506.8 2.0 gather_fusion.3
  508.7 0.1 gather.21
  508.9 1.3 reduce_sum.25
  (31 shorter events, 0.3 us)
Async XLA Ops:
  7.2 334.3 %copy-start = (bf16[1,192,4096]{2,1,0:T(8,128)(2,1)S(1)}, bf16[1,192,4096]{2,1,0:T(8,128)(2,1)}, u32[]{:S(2)}) copy-start(bf16[1,192,4096]{2,1,0:T(8,128)(2,1)} %param.11) | copy-start | bytes 4718596
  7.2 6.9 %copy-start.6 = (s32[128,4]{0,1:T(4,128)S(1)}, s32[128,4]{0,1:T(4,128)}, u32[]{:S(2)}) copy-start(s32[128,4]{0,1:T(4,128)} %param.8) | copy-start | bytes 6148
  7.2 8.9 %copy-start.7 = (bf16[128,4]{0,1:T(4,128)(2,1)S(1)}, bf16[128,4]{0,1:T(4,128)(2,1)}, u32[]{:S(2)}) copy-start(bf16[128,4]{0,1:T(4,128)(2,1)} %param.9) | copy-start | bytes 3076
  9.3 17.6 %all-to-all-start.1 = ((bf16[8,128,512]{2,1,0:T(8,128)(2,1)}), bf16[8,128,512]{2,1,0:T(8,128)(2,1)S(1)}, u32[]{:S(2)}, u32[]{:S(2)}) async-start(bf16[8,128,512]{2,1,0:T(8,128)(2,1)} %stack.8), calls=%async_computation.1 | async-start | bytes 2097152 | tf_op jit(solution)/shard_map/all_to_all | solution.py:11
  26.9 1.0 copy-start.3
  44.2 155.2 %all-to-all-start.2 = ((bf16[16,64,4096]{2,1,0:T(8,128)(2,1)}), bf16[16,64,4096]{2,1,0:T(8,128)(2,1)}, u32[]{:S(2)}, u32[]{:S(2)}) async-start(bf16[16,64,4096]{2,1,0:T(8,128)(2,1)} %broadcast_select_fusion), calls=%async_computation.2 | async-start | bytes 16777216 | tf_op jit(solution)/shard_map/all_to_all | solution.py:57
  52.1 26.8 %all-gather.2.cloned.1.call-start = ((), (), s32[]{:S(2)}) async-start(), calls=%async_computation.5 | async-start | bytes 1179648 | tf_op jit(solution)/shard_map/all_gather | solution.py:50
  199.4 142.1 %all-to-all-start = ((bf16[16,64,4096]{2,1,0:T(8,128)(2,1)}), bf16[16,64,4096]{2,1,0:T(8,128)(2,1)}, u32[]{:S(2)}, u32[]{:S(2)}) async-start(bf16[16,64,4096]{2,1,0:T(8,128)(2,1)} %fusion), calls=%async_computation | async-start | bytes 16777216 | tf_op jit(solution)/shard_map/all_to_all | solution.py:58
  207.8 276.5 %reduce-scatter.2.cloned.1.call-start = ((), (), s32[]{:S(2)}) async-start(), calls=%async_computation.6 | async-start | bytes 9437184 | tf_op jit(solution)/shard_map/reduce_scatter | solution.py:77
  208.0 6.9 %copy-start.4 = (bf16[1,2,192,4096]{3,2,1,0:T(8,128)(2,1)S(1)}, bf16[1,2,192,4096]{3,2,1,0:T(8,128)(2,1)}, u32[]{:S(2)}) copy-start(bf16[1,2,192,4096]{3,2,1,0:T(8,128)(2,1)} %param.10) | copy-start | bytes 9437188
  341.5 6.7 %copy-start.5 = (bf16[1,2,192,4096]{3,2,1,0:T(8,128)(2,1)S(1)}, bf16[1,2,192,4096]{3,2,1,0:T(8,128)(2,1)}, u32[]{:S(2)}) copy-start(bf16[1,2,192,4096]{3,2,1,0:T(8,128)(2,1)} %param.10) | copy-start | bytes 9437188
  373.2 5.8 %copy-start.1 = (bf16[1,1,192,4096]{3,2,1,0:T(8,128)(2,1)}, bf16[1,1,192,4096]{3,2,1,0:T(8,128)(2,1)S(1)}, u32[]{:S(2)}) copy-start(bf16[1,1,192,4096]{3,2,1,0:T(8,128)(2,1)S(1)} %fusion.1) | copy-start | bytes 4718596
  379.0 2.4 copy-start.2
  379.0 2.4 copy-start.8
  381.4 111.7 %collective-permute-start = (bf16[1,2,192,4096]{3,2,1,0:T(8,128)(2,1)}, bf16[1,2,192,4096]{3,2,1,0:T(8,128)(2,1)}, u32[]{:S(2)}, u32[]{:S(2)}) collective-permute-start(bf16[1,2,192,4096]{3,2,1,0:T(8,128)(2,1)} %pad_maximum_fusion), channel_id=1, source_target_pairs={{0,64},{64,0},{8,72},{72,8},{16,80},{80,16},{24,88},{88,24},{32,96... | collective-permute-start | bytes 9437192 | tf_op jit(solution)/shard_map/ppermute | solution.py:25
  386.7 95.8 %collective-permute-start.1 = (bf16[1,192,4096]{2,1,0:T(8,128)(2,1)S(1)}, bf16[1,192,4096]{2,1,0:T(8,128)(2,1)S(1)}, u32[]{:S(2)}, u32[]{:S(2)}) collective-permute-start(bf16[1,192,4096]{2,1,0:T(8,128)(2,1)S(1)} %fusion.3), channel_id=1, source_target_pairs={{0,64},{64,0},{8,72},{72,8},{16,80},{80,16},{24,88},{88,24},{32,96... | collective-permute-start | bytes 4718600 | tf_op jit(solution)/shard_map/ppermute | solution.py:25
  484.3 22.5 %all-to-all-start.3 = ((bf16[16,64,512]{2,1,0:T(8,128)(2,1)}), bf16[16,64,512]{2,1,0:T(8,128)(2,1)S(1)}, u32[]{:S(2)}, u32[]{:S(2)}) async-start(bf16[16,64,512]{2,1,0:T(8,128)(2,1)} %reduce-scatter.2.cloned.1.call-done), calls=%async_computation.4 | async-start | bytes 2097152 | tf_op jit(solution)/shard_map/all_to_all | solution.py:83
Sparse Core Ops, SparseCore 0:
  54.7 24.2 all-gather.1
  367.9 53.7 reduce-scatter.1
